TPU v7x, 512 devices: a whole 4x8x8 slice. The times are simulated.
512 devices in a mesh: ctx: 32 (over y, x_hi, core), head: 16 (over z, x_lo).
Axes of the slice: x: 4 (x_hi: 2, x_lo: 2; x = x_hi * 2 + x_lo), y: 8, z: 8, core: 2. Of those that a mesh axis runs over, the one named last changes fastest.
Arguments:
- queries: bfloat16 [8192, 4096], P('ctx', 'head'), may hold values from -13 to 13
- key_states: bfloat16 [8192, 2048], P('ctx', 'head'), may hold values from -12 to 12
- value_states: bfloat16 [8192, 2048], P('ctx', 'head'), may hold values from -6 to 6
- past_keys: bfloat16 [1024, 2048], P(None, 'head'), may hold values from -12 to 12
- past_values: bfloat16 [1024, 2048], P(None, 'head'), may hold values from -6 to 6
- out_weight: bfloat16 [4096, 5376], P('head'), may hold values from -0.125 to 0.125
Outputs:
- layer_output: bfloat16 [8192, 5376], P('ctx', 'head')
All inputs are finite; a program needn't handle non-finite values.
Results may differ from a plain program's by a relative error of at most 0.025.
Values may be sent and summed in bfloat16 or wider, within the bound.
A program may use at most 64 MiB of HBM per device.

v0:
```python
import jax
import jax.numpy as jnp
from jax import lax
from jax.sharding import PartitionSpec as P

HEAD_DIM = 128
WINDOW = 1024
QUERY_SCALAR = 168


def from_behind(x, axis, by):
    size = lax.axis_size(axis)
    pairs = [(i, i + by) for i in range(size) if 0 <= i + by < size]
    return lax.ppermute(x, axis, pairs)


def rounded(partial_term):
    return lax.optimization_barrier(partial_term.astype(jnp.bfloat16)).astype(jnp.float32)


def body(queries, key_states, value_states, past_keys, past_values, out_weight):
    block_rows = queries.shape[0]
    hop_count = past_keys.shape[0] // block_rows
    kv_local = key_states.shape[1] // HEAD_DIM
    group_size = queries.shape[1] // key_states.shape[1]
    window_rows = (hop_count + 1) * block_rows
    score_scale = QUERY_SCALAR ** (-0.5)
    position = lax.axis_index("ctx")
    received = []
    for distance in range(1, hop_count + 1):
        received.append(from_behind((key_states, value_states), "ctx", distance))
    key_parts = [key_states]
    value_parts = [value_states]
    for distance in range(1, hop_count + 1):
        earlier = position - distance
        past_start = jnp.maximum(earlier + hop_count, 0) * block_rows
        from_past = earlier < 0
        past_key_rows = lax.dynamic_slice_in_dim(past_keys, past_start, block_rows, 0)
        past_value_rows = lax.dynamic_slice_in_dim(past_values, past_start, block_rows, 0)
        key_parts.insert(0, jnp.where(from_past, past_key_rows, received[distance - 1][0]))
        value_parts.insert(0, jnp.where(from_past, past_value_rows, received[distance - 1][1]))
    window_keys = jnp.concatenate(key_parts, axis=0).reshape(window_rows, kv_local, HEAD_DIM)
    window_values = jnp.concatenate(value_parts, axis=0).reshape(window_rows, kv_local, HEAD_DIM)
    query_block = queries.reshape(block_rows, kv_local, group_size, HEAD_DIM)
    scores = (
        jnp.einsum("tkgd,skd->kgts", query_block, window_keys, preferred_element_type=jnp.float32)
        * score_scale
    )
    query_pos = position * block_rows + jnp.arange(block_rows, dtype=jnp.int32)
    key_pos = (position - hop_count) * block_rows + jnp.arange(window_rows, dtype=jnp.int32)
    distance_back = query_pos[:, None] - key_pos[None, :]
    visible = (distance_back >= 0) & (distance_back < WINDOW)
    scores = jnp.where(visible, scores, -jnp.inf)
    maxima = jnp.max(scores, axis=-1, keepdims=True)
    shifted = jnp.exp(scores - maxima)
    softmax_weights = (shifted / jnp.sum(shifted, axis=-1, keepdims=True)).astype(jnp.bfloat16)
    mixed_heads = jnp.einsum(
        "kgts,skd->tkgd", softmax_weights, window_values, preferred_element_type=jnp.float32
    )
    attended = mixed_heads.astype(jnp.bfloat16).reshape(block_rows, queries.shape[1])
    product = lax.dot_general(
        out_weight, attended, (((0,), (1,)), ((), ())), preferred_element_type=jnp.float32
    )
    summed = lax.psum_scatter(
        rounded(product).astype(jnp.bfloat16), "head", scatter_dimension=0, tiled=True
    )
    layer_output = summed.T
    return layer_output


def solution(mesh):
    placed = (
        P("ctx", "head"),
        P("ctx", "head"),
        P("ctx", "head"),
        P(None, "head"),
        P(None, "head"),
        P("head", None),
    )
    return jax.shard_map(
        body, mesh=mesh, in_specs=placed, out_specs=P("ctx", "head"), check_vma=False
    )
```

profile of v0, /device:TPU:8, one launch (start us, length us, event | category | flops | bytes accessed | tf_op | source)
XLA Modules:
  0.0 151.9 jit_solution(10213003233837378032)
XLA Ops:
  6.5 0.0 copy-start
  6.5 0.0 reduce-scatter.4.cloned.1.call-start
  6.5 5.2 %collective-permute-start.6 = (bf16[256,128]{1,0:T(8,128)(2,1)}, bf16[256,128]{1,0:T(8,128)(2,1)S(1)}, u32[]{:S(2)}, u32[]{:S(2)}) collective-permute-start(bf16[256,128]{1,0:T(8,128)(2,1)} %param.7), channel_id=1, source_target_pairs={{0,32},{16,48},{32,64},{48,80},{64,96},{80,112},{96,128},{112,144}... | collective-permute-start | bytes 196616 | tf_op jit(solution)/shard_map/ppermute | solution.py:14
  11.7 2.6 %collective-permute-start.5 = (bf16[256,128]{1,0:T(8,128)(2,1)}, bf16[256,128]{1,0:T(8,128)(2,1)S(1)}, u32[]{:S(2)}, u32[]{:S(2)}) collective-permute-start(bf16[256,128]{1,0:T(8,128)(2,1)} %param.7), channel_id=1, source_target_pairs={{0,48},{16,64},{32,80},{48,96},{64,112},{80,128},{96,144},{112,160... | collective-permute-start | bytes 196616 | tf_op jit(solution)/shard_map/ppermute | solution.py:14
  14.3 3.5 %collective-permute-start.4 = (bf16[256,128]{1,0:T(8,128)(2,1)}, bf16[256,128]{1,0:T(8,128)(2,1)S(1)}, u32[]{:S(2)}, u32[]{:S(2)}) collective-permute-start(bf16[256,128]{1,0:T(8,128)(2,1)} %param.7), channel_id=1, source_target_pairs={{0,64},{16,80},{32,96},{48,112},{64,128},{80,144},{96,160},{112,17... | collective-permute-start | bytes 196616 | tf_op jit(solution)/shard_map/ppermute | solution.py:14
  17.8 2.6 %collective-permute-start.7 = (bf16[256,128]{1,0:T(8,128)(2,1)}, bf16[256,128]{1,0:T(8,128)(2,1)S(1)}, u32[]{:S(2)}, u32[]{:S(2)}) collective-permute-start(bf16[256,128]{1,0:T(8,128)(2,1)} %param.7), channel_id=1, source_target_pairs={{0,16},{16,32},{32,48},{48,64},{64,80},{80,96},{96,112},{112,128},... | collective-permute-start | bytes 196616 | tf_op jit(solution)/shard_map/ppermute | solution.py:14
  20.5 4.7 %collective-permute-start = (bf16[256,128]{1,0:T(8,128)(2,1)}, bf16[256,128]{1,0:T(8,128)(2,1)S(1)}, u32[]{:S(2)}, u32[]{:S(2)}) collective-permute-start(bf16[256,128]{1,0:T(8,128)(2,1)} %param.8), channel_id=1, source_target_pairs={{0,64},{16,80},{32,96},{48,112},{64,128},{80,144},{96,160},{112,17... | collective-permute-start | bytes 196616 | tf_op jit(solution)/shard_map/ppermute | solution.py:14
  25.2 0.4 fusion.6
  25.6 1.8 %collective-permute-done = bf16[256,128]{1,0:T(8,128)(2,1)S(1)} collective-permute-done((bf16[256,128]{1,0:T(8,128)(2,1)}, bf16[256,128]{1,0:T(8,128)(2,1)S(1)}, u32[]{:S(2)}, u32[]{:S(2)}) %collective-permute-start) | collective-permute-done | bytes 65568 | tf_op jit(solution)/shard_map/ppermute | solution.py:14
  27.4 4.8 %collective-permute-start.2 = (bf16[256,128]{1,0:T(8,128)(2,1)}, bf16[256,128]{1,0:T(8,128)(2,1)S(1)}, u32[]{:S(2)}, u32[]{:S(2)}) collective-permute-start(bf16[256,128]{1,0:T(8,128)(2,1)} %param.8), channel_id=1, source_target_pairs={{0,32},{16,48},{32,64},{48,80},{64,96},{80,112},{96,128},{112,144}... | collective-permute-start | bytes 196616 | tf_op jit(solution)/shard_map/ppermute | solution.py:14
  32.2 0.9 select_dynamic-update-slice_fusion.7
  33.0 0.0 collective-permute-done.4
  33.0 4.8 %collective-permute-start.1 = (bf16[256,128]{1,0:T(8,128)(2,1)}, bf16[256,128]{1,0:T(8,128)(2,1)S(1)}, u32[]{:S(2)}, u32[]{:S(2)}) collective-permute-start(bf16[256,128]{1,0:T(8,128)(2,1)} %param.8), channel_id=1, source_target_pairs={{0,48},{16,64},{32,80},{48,96},{64,112},{80,128},{96,144},{112,160... | collective-permute-start | bytes 196616 | tf_op jit(solution)/shard_map/ppermute | solution.py:14
  37.9 0.9 select_dynamic-update-slice_fusion.3
  38.8 1.3 collective-permute-done.1
  40.1 3.4 %collective-permute-start.3 = (bf16[256,128]{1,0:T(8,128)(2,1)}, bf16[256,128]{1,0:T(8,128)(2,1)S(1)}, u32[]{:S(2)}, u32[]{:S(2)}) collective-permute-start(bf16[256,128]{1,0:T(8,128)(2,1)} %param.8), channel_id=1, source_target_pairs={{0,16},{16,32},{32,48},{48,64},{64,80},{80,96},{96,112},{112,128},... | collective-permute-start | bytes 196616 | tf_op jit(solution)/shard_map/ppermute | solution.py:14
  43.5 0.9 select_dynamic-update-slice_fusion.6
  44.3 0.0 collective-permute-done.5
  44.3 0.9 select_dynamic-update-slice_fusion.2
  45.2 0.0 collective-permute-done.2
  45.2 0.9 select_dynamic-update-slice_fusion.5
  46.1 0.0 collective-permute-done.6
  46.1 0.9 select_dynamic-update-slice_fusion.1
  47.0 0.0 collective-permute-done.7
  47.0 1.3 collective-permute-done.3
  48.3 0.9 select_dynamic-update-slice_fusion
  49.2 0.9 constant_dynamic-update-slice_fusion.1
  50.1 0.9 constant_dynamic-update-slice_fusion
  50.9 1.4 fusion.14
  52.3 0.4 fusion.3
  52.7 0.6 fusion.7
  53.3 0.0 copy-done
  53.3 2.5 %fusion = bf16[5376,256]{0,1:T(8,128)(2,1)} fusion(bf16[256,256]{0,1:T(8,128)(2,1)S(1)} %bitcast.40, bf16[256,5376]{1,0:T(8,128)(2,1)S(1)} %copy-done), kind=kOutput, calls=%fused_computation.1 | convolution fusion | flops 706019328 | bytes 5636096 | tf_op jit(solution)/shard_map/dot_general | solution.py:61
  55.8 4.6 %copy.18 = bf16[5376,256]{1,0:T(8,128)(2,1)} copy(bf16[5376,256]{0,1:T(8,128)(2,1)} %fusion) | data formatting | bytes 5505024
  60.4 0.0 reduce-scatter.4.cloned.1.call-update
  60.5 84.6 %reduce-scatter.4.cloned.1.call-done = bf16[336,256]{1,0:T(8,128)(2,1)} async-done(((bf16[5376,256]{1,0:T(8,128)(2,1)}), bf16[336,256]{1,0:T(8,128)(2,1)}) %reduce-scatter.4.cloned.1.call-update) | async-done | bytes 172048
  (2 shorter events, 0.0 us)
Async XLA Ops:
  6.5 46.8 %copy-start = (bf16[256,5376]{1,0:T(8,128)(2,1)S(1)}, bf16[256,5376]{1,0:T(8,128)(2,1)}, u32[]{:S(2)}) copy-start(bf16[256,5376]{1,0:T(8,128)(2,1)} %param.11) | copy-start | bytes 8257540
  6.5 138.5 %reduce-scatter.4.cloned.1.call-start = ((), (), s32[]{:S(2)}) async-start(), calls=%async_computation.1 | async-start | bytes 2924544
  6.5 39.6 %collective-permute-start.6 = (bf16[256,128]{1,0:T(8,128)(2,1)}, bf16[256,128]{1,0:T(8,128)(2,1)S(1)}, u32[]{:S(2)}, u32[]{:S(2)}) collective-permute-start(bf16[256,128]{1,0:T(8,128)(2,1)} %param.7), channel_id=1, source_target_pairs={{0,32},{16,48},{32,64},{48,80},{64,96},{80,112},{96,128},{112,144}... | collective-permute-start | bytes 196616 | tf_op jit(solution)/shard_map/ppermute | solution.py:14
  11.7 32.6 %collective-permute-start.5 = (bf16[256,128]{1,0:T(8,128)(2,1)}, bf16[256,128]{1,0:T(8,128)(2,1)S(1)}, u32[]{:S(2)}, u32[]{:S(2)}) collective-permute-start(bf16[256,128]{1,0:T(8,128)(2,1)} %param.7), channel_id=1, source_target_pairs={{0,48},{16,64},{32,80},{48,96},{64,112},{80,128},{96,144},{112,160... | collective-permute-start | bytes 196616 | tf_op jit(solution)/shard_map/ppermute | solution.py:14
  14.3 18.7 %collective-permute-start.4 = (bf16[256,128]{1,0:T(8,128)(2,1)}, bf16[256,128]{1,0:T(8,128)(2,1)S(1)}, u32[]{:S(2)}, u32[]{:S(2)}) collective-permute-start(bf16[256,128]{1,0:T(8,128)(2,1)} %param.7), channel_id=1, source_target_pairs={{0,64},{16,80},{32,96},{48,112},{64,128},{80,144},{96,160},{112,17... | collective-permute-start | bytes 196616 | tf_op jit(solution)/shard_map/ppermute | solution.py:14
  17.8 29.2 %collective-permute-start.7 = (bf16[256,128]{1,0:T(8,128)(2,1)}, bf16[256,128]{1,0:T(8,128)(2,1)S(1)}, u32[]{:S(2)}, u32[]{:S(2)}) collective-permute-start(bf16[256,128]{1,0:T(8,128)(2,1)} %param.7), channel_id=1, source_target_pairs={{0,16},{16,32},{32,48},{48,64},{64,80},{80,96},{96,112},{112,128},... | collective-permute-start | bytes 196616 | tf_op jit(solution)/shard_map/ppermute | solution.py:14
  20.5 6.9 %collective-permute-start = (bf16[256,128]{1,0:T(8,128)(2,1)}, bf16[256,128]{1,0:T(8,128)(2,1)S(1)}, u32[]{:S(2)}, u32[]{:S(2)}) collective-permute-start(bf16[256,128]{1,0:T(8,128)(2,1)} %param.8), channel_id=1, source_target_pairs={{0,64},{16,80},{32,96},{48,112},{64,128},{80,144},{96,160},{112,17... | collective-permute-start | bytes 196616 | tf_op jit(solution)/shard_map/ppermute | solution.py:14
  27.4 17.8 %collective-permute-start.2 = (bf16[256,128]{1,0:T(8,128)(2,1)}, bf16[256,128]{1,0:T(8,128)(2,1)S(1)}, u32[]{:S(2)}, u32[]{:S(2)}) collective-permute-start(bf16[256,128]{1,0:T(8,128)(2,1)} %param.8), channel_id=1, source_target_pairs={{0,32},{16,48},{32,64},{48,80},{64,96},{80,112},{96,128},{112,144}... | collective-permute-start | bytes 196616 | tf_op jit(solution)/shard_map/ppermute | solution.py:14
  33.0 7.1 %collective-permute-start.1 = (bf16[256,128]{1,0:T(8,128)(2,1)}, bf16[256,128]{1,0:T(8,128)(2,1)S(1)}, u32[]{:S(2)}, u32[]{:S(2)}) collective-permute-start(bf16[256,128]{1,0:T(8,128)(2,1)} %param.8), channel_id=1, source_target_pairs={{0,48},{16,64},{32,80},{48,96},{64,112},{80,128},{96,144},{112,160... | collective-permute-start | bytes 196616 | tf_op jit(solution)/shard_map/ppermute | solution.py:14
  40.1 8.2 %collective-permute-start.3 = (bf16[256,128]{1,0:T(8,128)(2,1)}, bf16[256,128]{1,0:T(8,128)(2,1)S(1)}, u32[]{:S(2)}, u32[]{:S(2)}) collective-permute-start(bf16[256,128]{1,0:T(8,128)(2,1)} %param.8), channel_id=1, source_target_pairs={{0,16},{16,32},{32,48},{48,64},{64,80},{80,96},{96,112},{112,128},... | collective-permute-start | bytes 196616 | tf_op jit(solution)/shard_map/ppermute | solution.py:14
Sparse Core Ops, SparseCore 0:
  60.6 84.4 reduce-scatter.3
where the time goes:
time: 153 us; the launch traced here: 152 us
  waiting for transfers between devices  89 us (58%)
  starting transfers between devices  31.6 us (21%)
  between operations  13.6 us (9%)
  other arithmetic  6.92 us (5%)
  local copies, waits for them, and re-layouts  6.32 us (4%)
  matrix products  4.52 us (3%)
    unnamed x2, waiting for transfers between devices  84.6 us
    ppermute x8, starting transfers between devices, from_behind(): return lax.ppermute(x, axis, pairs)  31.6 us
    unnamed x7, other arithmetic  6.18 us
    unnamed x3, local copies, waits for them, and re-layouts  4.62 us
    ppermute x8, waiting for transfers between devices, from_behind(): return lax.ppermute(x, axis, pairs)  4.39 us
  transfers between devices with their start and end apart: 9, of which 4 were waited for; matrix products, arithmetic and copies ran while one was open for 4% of the time, Pallas kernels for 0%

commit v1 on v0

v1 whole, which is shorter than its diff:
```python
import functools

import jax
import jax.numpy as jnp
from jax import lax
from jax.experimental import pallas as pl
from jax.experimental.pallas import tpu as pltpu
from jax.sharding import PartitionSpec as P

HEAD_DIM = 128
QUERY_SCALAR = 168
LOG2E = 1.4426950408889634
NZ = 8
NY = 8
BLK = 256
HALF = 128
KEYS = 5 * BLK
SPAN = 1024 + HALF
COLS = 336
PAD = 384
ROWS = 16
MESH = pl.DeviceIdType.MESH
DIST = (0, 1, -1, 2, -2, 3, -3, 4)
SLOT = {d: i for i, d in enumerate(DIST)}


def kernel(
    q_hbm, k_hbm, v_hbm, pk_hbm, pv_hbm, w_hbm, o_hbm,
    q, kv, wrow, wsrc, wfull, att, acc, xsend, xrecv, out,
    in_sem, past_sem, out_sem,
    kv_send, kv_recv, fwd_send,
    w1_send, w1_recv, wy_send, wy_recv, ws_send, ws_recv,
    z_send, z_recv, x_send, x_recv,
):
    c = lax.axis_index("ctx")
    h = lax.axis_index("head")
    n_ctx = lax.axis_size("ctx")
    core = lax.rem(c, 2)
    y = c // 4
    z = h // 2
    x_lo = lax.rem(h, 2)
    sibling = (c + 1 - 2 * core, h)
    partner = (c, h + 1 - 2 * x_lo)

    def at_z(d):
        return (c, lax.rem(z + d + NZ, NZ) * 2 + x_lo)

    def at_c(d):
        return (lax.rem(c + d + n_ctx, n_ctx), h)

    my_w = pl.ds(pl.multiple_of(y * 32 + core * ROWS, ROWS), ROWS)
    loads = [
        pltpu.make_async_copy(k_hbm, kv.at[0, pl.ds(4 * BLK, BLK)], in_sem.at[0]),
        pltpu.make_async_copy(v_hbm, kv.at[1, pl.ds(4 * BLK, BLK)], in_sem.at[1]),
        pltpu.make_async_copy(w_hbm.at[my_w], wrow, in_sem.at[2]),
        pltpu.make_async_copy(q_hbm, q, in_sem.at[3]),
    ]
    for copy in loads:
        copy.start()

    def past_copies(j):
        rows = pl.ds(pl.multiple_of(jnp.minimum(c + j, 3) * BLK, BLK), BLK)
        return (
            pltpu.make_async_copy(pk_hbm.at[rows], kv.at[0, pl.ds(j * BLK, BLK)], past_sem.at[2 * j]),
            pltpu.make_async_copy(pv_hbm.at[rows], kv.at[1, pl.ds(j * BLK, BLK)], past_sem.at[2 * j + 1]),
        )

    for j in range(4):
        @pl.when(c + j < 4)
        def _(j=j):
            for copy in past_copies(j):
                copy.start()

    barrier = pltpu.get_barrier_semaphore()
    partners = [at_z(d) for d in range(1, NZ)] + [at_c(d) for d in (-4, -2, 2, 4)] + [sibling, partner]
    for device in partners:
        pl.semaphore_signal(barrier, inc=1, device_id=device, device_id_type=MESH)

    loads[2].wait()
    fill = jnp.zeros((ROWS, PAD - COLS), jnp.bfloat16)
    for t in range(NZ):
        at = t * 2 * COLS
        wsrc[t] = jnp.concatenate(
            [wrow[:, at : at + COLS], fill, wrow[:, at + COLS : at + 2 * COLS], fill], axis=1
        )
    loads[0].wait()
    loads[1].wait()
    pl.semaphore_wait(barrier, len(partners))

    def remote(src, dst, send, recv, device):
        return pltpu.make_async_remote_copy(
            src_ref=src, dst_ref=dst, send_sem=send, recv_sem=recv, device_id=device, device_id_type=MESH
        )

    def kv_slot(j):
        return kv.at[:, pl.ds(pl.multiple_of(j * BLK, BLK), BLK)]

    def kv_copy(j, device, send):
        return remote(kv_slot(4), kv_slot(j), send, kv_recv.at[j], device)

    to_far = kv_copy(0, at_c(4), kv_send.at[0])
    to_near = kv_copy(2, at_c(2), kv_send.at[1])
    to_next = kv_copy(3, sibling, kv_send.at[2])

    @pl.when(c + 2 < n_ctx)
    def _():
        to_near.start()

    @pl.when(c + 4 < n_ctx)
    def _():
        to_far.start()

    @pl.when(core == 0)
    def _():
        to_next.start()

    def w1_copy(d):
        target = lax.rem(z - d + NZ, NZ)
        s = SLOT[d]
        return remote(wsrc.at[target], wfull.at[s, my_w], w1_send.at[s], w1_recv.at[s], at_z(-d))

    for d in DIST[1:]:
        w1_copy(d).start()
    wfull[0, my_w] = wsrc[z]

    near_slot = jnp.where(core == 0, 1, 3)
    fwd_near = remote(kv_slot(2), kv_slot(near_slot), fwd_send.at[0], kv_recv.at[near_slot], sibling)
    fwd_far = remote(kv_slot(0), kv_slot(1), fwd_send.at[1], kv_recv.at[1], sibling)

    def arrived(j):
        return remote(kv_slot(j), kv_slot(j), kv_send.at[0], kv_recv.at[j], sibling)

    @pl.when(c >= 4)
    def _():
        arrived(0).wait_recv()

    @pl.when((c >= 4) & (core == 1))
    def _():
        fwd_far.start()

    @pl.when(c >= 2)
    def _():
        arrived(2).wait_recv()
        fwd_near.start()

    def w_slab(part, dy, of_core):
        row = pl.multiple_of(lax.rem(y + dy + NY, NY) * 32 + of_core * ROWS, ROWS)
        return wfull.at[pl.ds(part * 4, 4), pl.ds(row, ROWS)]

    def wy_copy(part, way, step):
        slab = w_slab(part, -way * (step - 1), core)
        i = part * 8 + (way + 1) // 2 * 4 + step - 1
        return remote(slab, slab, wy_send.at[i], wy_recv.at[i], at_c(4 * way))

    def wy_arrived(part, way, step):
        slab = w_slab(part, -way * step, core)
        i = part * 8 + (way + 1) // 2 * 4 + step - 1
        return remote(slab, slab, wy_send.at[i], wy_recv.at[i], at_c(4 * way))

    def ws_copy(part, dy):
        slab = w_slab(part, dy, core)
        i = part * 8 + dy + 3
        return remote(slab, slab, ws_send.at[i], ws_recv.at[i], sibling)

    def ws_arrived(part, dy):
        slab = w_slab(part, dy, 1 - core)
        i = part * 8 + dy + 3
        return remote(slab, slab, ws_send.at[i], ws_recv.at[i], sibling)

    def last_way(part):
        return 1 if part == 0 else -1

    def w_start():
        for part in range(2):
            for s in range(max(1, part * 4), part * 4 + 4):
                w1_copy(DIST[s]).wait_recv()
            for way in (1, -1):
                wy_copy(part, way, 1).start()
            ws_copy(part, 0).start()

    def w_step(part, step):
        for way in (1, -1):
            if step == 4 and way != last_way(part):
                continue
            wy_arrived(part, way, step).wait_recv()
            if step < 3 or (step == 3 and way == last_way(part)):
                wy_copy(part, way, step + 1).start()
            ws_copy(part, 4 if step == 4 else -way * step).start()

    w_start()

    for j in range(4):
        @pl.when(c + j < 4)
        def _(j=j):
            for copy in past_copies(j):
                copy.wait()

    loads[3].wait()

    @pl.when((c >= 1) | (core == 1))
    def _():
        arrived(3).wait_recv()

    @pl.when(c >= 3)
    def _():
        arrived(1).wait_recv()

    factor = QUERY_SCALAR ** (-0.5) * LOG2E
    row = lax.broadcasted_iota(jnp.int32, (HALF, HALF), 0)
    col = lax.broadcasted_iota(jnp.int32, (HALF, HALF), 1)

    def attend(half):
        rows = pl.ds(half * HALF, HALF)
        keys = kv[0, half * HALF : half * HALF + SPAN]
        values = kv[1, half * HALF : half * HALF + SPAN]
        for g in range(2):
            head = pl.ds(g * HEAD_DIM, HEAD_DIM)
            s = lax.dot_general(
                q[rows, head], keys, (((1,), (1,)), ((), ())), preferred_element_type=jnp.float32
            )
            s = jnp.concatenate(
                [
                    jnp.where(col > row, s[:, :HALF], -jnp.inf),
                    s[:, HALF : SPAN - HALF],
                    jnp.where(col <= row, s[:, SPAN - HALF :], -jnp.inf),
                ],
                axis=1,
            )
            m = jnp.max(s, axis=1, keepdims=True)
            p = jnp.exp2((s - m) * factor)
            total = jnp.sum(p, axis=1, keepdims=True)
            mixed = jnp.dot(p.astype(jnp.bfloat16), values, preferred_element_type=jnp.float32)
            att[0, rows, head] = (mixed / total).astype(jnp.bfloat16)

    def z_copy(half, way, step):
        src, dst = SLOT[-way * (step - 1)], SLOT[4 if step == 4 else -way * step]
        rows = pl.ds(half * HALF, HALF)
        i = half * 8 + (way + 1) // 2 * 4 + step - 1
        return remote(att.at[src, rows], att.at[dst, rows], z_send.at[i], z_recv.at[i], at_z(way))

    def z_step(half, step):
        for way in (1, -1):
            if step == 4 and way != last_way(half):
                continue
            z_copy(half, way, step).wait_recv()
            if step < 3 or (step == 3 and way == last_way(half)):
                z_copy(half, way, step + 1).start()

    for half in range(2):
        attend(half)
        for way in (1, -1):
            z_copy(half, way, 1).start()

    w_step(0, 1)
    w_step(1, 1)
    z_step(0, 1)
    z_step(1, 1)
    z_step(0, 2)
    w_step(0, 2)
    z_step(1, 2)
    w_step(1, 2)
    z_step(0, 3)
    w_step(0, 3)
    z_step(1, 3)
    w_step(1, 3)

    def project(half, slots, first):
        rows = pl.ds(half * HALF, HALF)
        for s in slots:
            term = jnp.dot(att[s, rows, :], wfull[s], preferred_element_type=jnp.float32)
            if first and s == slots[0]:
                acc[rows, :] = term
            else:
                acc[rows, :] += term

    w_step(0, 4)
    w_step(1, 4)
    for part in range(2):
        for dy in range(-3, 5):
            ws_arrived(part, dy).wait_recv()

    def x_copy(half):
        rows = pl.ds(half * HALF, HALF)
        return remote(xsend.at[rows], xrecv.at[rows], x_send.at[half], x_recv.at[half], partner)

    mine = pl.ds(pl.multiple_of(x_lo * PAD, PAD), PAD)
    theirs = pl.ds(pl.multiple_of((1 - x_lo) * PAD, PAD), PAD)
    for half in range(2):
        rows = pl.ds(half * HALF, HALF)
        project(half, range(7), True)
        z_step(half, 4)
        project(half, range(7, 8), False)
        xsend[rows, :] = acc[rows, theirs].astype(jnp.bfloat16)
        x_copy(half).start()
    stores = []
    for half in range(2):
        rows = pl.ds(half * HALF, HALF)
        x_copy(half).wait_recv()
        both = acc[rows, mine] + xrecv[rows, :].astype(jnp.float32)
        out[rows, :] = both[:, :COLS].astype(jnp.bfloat16)
        store = pltpu.make_async_copy(out.at[rows], o_hbm.at[rows], out_sem.at[half])
        store.start()
        stores.append(store)

    @pl.when(c + 2 < n_ctx)
    def _():
        to_near.wait_send()

    @pl.when(c + 4 < n_ctx)
    def _():
        to_far.wait_send()

    @pl.when(core == 0)
    def _():
        to_next.wait_send()

    @pl.when(c >= 2)
    def _():
        fwd_near.wait_send()

    @pl.when((c >= 4) & (core == 1))
    def _():
        fwd_far.wait_send()

    for d in DIST[1:]:
        w1_copy(d).wait_send()
    for part in range(2):
        for way in (1, -1):
            for step in range(1, 5):
                if step < 4 or way == last_way(part):
                    wy_copy(part, way, step).wait_send()
                    z_copy(part, way, step).wait_send()
        for dy in range(-3, 5):
            ws_copy(part, dy).wait_send()
        x_copy(part).wait_send()
    for store in stores:
        store.wait()


def body(queries, key_states, value_states, past_keys, past_values, out_weight):
    bf16 = jnp.bfloat16
    dma = pltpu.SemaphoreType.DMA
    return pl.pallas_call(
        kernel,
        out_shape=jax.ShapeDtypeStruct((BLK, COLS), bf16),
        in_specs=[pl.BlockSpec(memory_space=pl.ANY)] * 6,
        out_specs=pl.BlockSpec(memory_space=pl.ANY),
        scratch_shapes=[
            pltpu.VMEM((BLK, 2 * HEAD_DIM), bf16),
            pltpu.VMEM((2, KEYS, HEAD_DIM), bf16),
            pltpu.VMEM((ROWS, out_weight.shape[1]), bf16),
            pltpu.VMEM((NZ, ROWS, 2 * PAD), bf16),
            pltpu.VMEM((NZ, BLK, 2 * PAD), bf16),
            pltpu.VMEM((NZ, BLK, 2 * HEAD_DIM), bf16),
            pltpu.VMEM((BLK, 2 * PAD), jnp.float32),
            pltpu.VMEM((BLK, PAD), bf16),
            pltpu.VMEM((BLK, PAD), bf16),
            pltpu.VMEM((BLK, COLS), bf16),
            dma((4,)), dma((8,)), dma((2,)),
            dma((3,)), dma((4,)), dma((2,)),
            dma((8,)), dma((8,)), dma((16,)), dma((16,)), dma((16,)), dma((16,)),
            dma((16,)), dma((16,)), dma((2,)), dma((2,)),
        ],
        compiler_params=pltpu.CompilerParams(
            collective_id=0, has_side_effects=True, vmem_limit_bytes=48 * 1024 * 1024
        ),
        cost_estimate=pl.CostEstimate(flops=10**9, bytes_accessed=4 * 10**6, transcendentals=700000),
    )(queries, key_states, value_states, past_keys, past_values, out_weight)


def solution(mesh):
    placed = (
        P("ctx", "head"),
        P("ctx", "head"),
        P("ctx", "head"),
        P(None, "head"),
        P(None, "head"),
        P("head", None),
    )
    return jax.shard_map(
        body, mesh=mesh, in_specs=placed, out_specs=P("ctx", "head"), check_vma=False
    )
```

time: 153 us -> 56.9 us (0.37)
  the two profiles are of different devices: /device:TPU:8 before, /device:TPU:21 now
where the time goes in v1:
time: 56.9 us; the launch traced here: 56.6 us
  Pallas kernels  49.5 us (87%)
  local copies, waits for them, and re-layouts  7.06 us (12%)
    pallas_call x1, Pallas kernels, body(): pl.pallas_call(kernel, out_shape=jax.ShapeDtypeStruct((BLK, COLS), bf16),...  49.5 us
    unnamed x12, local copies, waits for them, and re-layouts  6.26 us

profile of v1, /device:TPU:21, one launch (start us, length us, event | category | flops | bytes accessed | tf_op | source)
XLA Modules:
  0.0 56.6 jit_solution(10078871688539344214)
XLA Ops:
  0.0 0.0 copy-start
  0.0 1.8 %copy-done = bf16[256,5376]{1,0:T(8,128)(2,1)S(1)} copy-done((bf16[256,5376]{1,0:T(8,128)(2,1)S(1)}, bf16[256,5376]{1,0:T(8,128)(2,1)}, u32[]{:S(2)}) %copy-start) | copy-done | bytes 2752536
  1.8 0.0 copy-start.1
  1.8 0.9 %copy-done.1 = bf16[1024,128]{1,0:T(8,128)(2,1)S(1)} copy-done((bf16[1024,128]{1,0:T(8,128)(2,1)S(1)}, bf16[1024,128]{1,0:T(8,128)(2,1)}, u32[]{:S(2)}) %copy-start.1) | copy-done | bytes 262168
  2.7 0.0 copy-start.2
  2.7 0.9 %copy-done.2 = bf16[1024,128]{1,0:T(8,128)(2,1)S(1)} copy-done((bf16[1024,128]{1,0:T(8,128)(2,1)S(1)}, bf16[1024,128]{1,0:T(8,128)(2,1)}, u32[]{:S(2)}) %copy-start.2) | copy-done | bytes 262168
  3.7 0.0 copy-start.3
  3.7 0.9 %copy-done.3 = bf16[256,256]{1,0:T(8,128)(2,1)S(1)} copy-done((bf16[256,256]{1,0:T(8,128)(2,1)S(1)}, bf16[256,256]{1,0:T(8,128)(2,1)}, u32[]{:S(2)}) %copy-start.3) | copy-done | bytes 131096
  4.6 0.0 copy-start.4
  4.6 0.8 %copy-done.4 = bf16[256,128]{1,0:T(8,128)(2,1)S(1)} copy-done((bf16[256,128]{1,0:T(8,128)(2,1)S(1)}, bf16[256,128]{1,0:T(8,128)(2,1)}, u32[]{:S(2)}) %copy-start.4) | copy-done | bytes 65560
  5.4 0.0 copy-start.5
  5.4 0.8 %copy-done.5 = bf16[256,128]{1,0:T(8,128)(2,1)S(1)} copy-done((bf16[256,128]{1,0:T(8,128)(2,1)S(1)}, bf16[256,128]{1,0:T(8,128)(2,1)}, u32[]{:S(2)}) %copy-start.5) | copy-done | bytes 65560
  6.3 49.5 %shard_map.64 = bf16[256,336]{1,0:T(8,128)(2,1)S(1)} custom-call(bf16[256,256]{1,0:T(8,128)(2,1)S(1)} %copy-done.3, bf16[256,128]{1,0:T(8,128)(2,1)S(1)} %copy-done.4, bf16[256,128]{1,0:T(8,128)(2,1)S(1)} %copy-done.5, bf16[1024,128]{1,0:T(8,128)(2,1)S(1)} %copy-done.1, bf16[1024,128]{1,0:T(8,128)(2,1)S(1)} %copy-done.2, bf16[256,5376]{1,0:T(8,128)(2,1)S(1)} %copy-done), custom_call_target="tpu_custom_call" | custom-call | flops 1000000000 | bytes 4000000 | tf_op jit(solution)/shard_map/pallas_call | solution.py:343
  55.8 0.8 %copy.7 = bf16[256,336]{0,1:T(8,128)(2,1)} copy(bf16[256,336]{1,0:T(8,128)(2,1)S(1)} %shard_map.64) | data formatting | bytes 344064 | tf_op jit(solution)/shard_map/pallas_call | solution.py:343
Async XLA Ops:
  0.0 1.8 %copy-start = (bf16[256,5376]{1,0:T(8,128)(2,1)S(1)}, bf16[256,5376]{1,0:T(8,128)(2,1)}, u32[]{:S(2)}) copy-start(bf16[256,5376]{1,0:T(8,128)(2,1)} %w_hbm.1) | copy-start | bytes 8257540
  1.8 0.9 %copy-start.1 = (bf16[1024,128]{1,0:T(8,128)(2,1)S(1)}, bf16[1024,128]{1,0:T(8,128)(2,1)}, u32[]{:S(2)}) copy-start(bf16[1024,128]{1,0:T(8,128)(2,1)} %pk_hbm.1) | copy-start | bytes 786436
  2.7 0.9 %copy-start.2 = (bf16[1024,128]{1,0:T(8,128)(2,1)S(1)}, bf16[1024,128]{1,0:T(8,128)(2,1)}, u32[]{:S(2)}) copy-start(bf16[1024,128]{1,0:T(8,128)(2,1)} %pv_hbm.1) | copy-start | bytes 786436
  3.7 0.9 %copy-start.3 = (bf16[256,256]{1,0:T(8,128)(2,1)S(1)}, bf16[256,256]{1,0:T(8,128)(2,1)}, u32[]{:S(2)}) copy-start(bf16[256,256]{1,0:T(8,128)(2,1)} %q_hbm.1) | copy-start | bytes 393220
  4.6 0.8 %copy-start.4 = (bf16[256,128]{1,0:T(8,128)(2,1)S(1)}, bf16[256,128]{1,0:T(8,128)(2,1)}, u32[]{:S(2)}) copy-start(bf16[256,128]{1,0:T(8,128)(2,1)} %k_hbm.1) | copy-start | bytes 196612
  5.4 0.8 %copy-start.5 = (bf16[256,128]{1,0:T(8,128)(2,1)S(1)}, bf16[256,128]{1,0:T(8,128)(2,1)}, u32[]{:S(2)}) copy-start(bf16[256,128]{1,0:T(8,128)(2,1)} %v_hbm.1) | copy-start | bytes 196612

commit v2 on v0

v2 whole, which is shorter than its diff:
```python
import jax
import jax.numpy as jnp
from jax import lax
from jax.experimental import pallas as pl
from jax.experimental.pallas import tpu as pltpu
from jax.sharding import PartitionSpec as P

HEAD_DIM = 128
QUERY_SCALAR = 168
LOG2E = 1.4426950408889634
NZ = 8
NY = 8
BLK = 256
HALF = 128
CHUNKS = 4
CHUNK = BLK // CHUNKS
KEYS = 5 * BLK
SPAN = 1024 + HALF
COLS = 336
TILES = 21
MAIN = 640
TAIL = 32
ROWS = 16
MESH = pl.DeviceIdType.MESH
DIST = (0, 1, -1, 2, -2, 3, -3, 4)
SLOT = {d: i for i, d in enumerate(DIST)}


def kernel(
    q_hbm, k_hbm, v_hbm, pk_hbm, pv_hbm, w_hbm, own_hbm, other_hbm,
    q, kv, wrow, wsrc, wstage, wfull, att, acc, acc_t, xsend,
    in_sem, past_sem, own_sem, kv_send, kv_recv, fwd_send,
    w1_send, w1_recv, wy_send, wy_recv, ws_send, ws_recv,
    z1_send, z1_recv, z_send, z_recv, z4_send, z4_recv, zs_send, zs_recv, x_send, x_recv,
):
    c = lax.axis_index("ctx")
    h = lax.axis_index("head")
    n_ctx = lax.axis_size("ctx")
    core = lax.rem(c, 2)
    c0 = c - core
    y = c // 4
    z = h // 2
    x_lo = lax.rem(h, 2)
    sibling = (c + 1 - 2 * core, h)
    partner = (c, h + 1 - 2 * x_lo)

    def at_z(d, of_core):
        return (c0 + of_core, lax.rem(z + d + NZ, NZ) * 2 + x_lo)

    def at_c(d):
        return (lax.rem(c + d + n_ctx, n_ctx), h)

    barrier = pltpu.get_barrier_semaphore()

    def greet(devices):
        for device in devices:
            pl.semaphore_signal(barrier, inc=1, device_id=device, device_id_type=MESH)

    def on_core(which):
        return pl.when(core == which)

    my_w = pl.ds(pl.multiple_of(y * 32 + core * ROWS, ROWS), ROWS)
    loads = [
        pltpu.make_async_copy(w_hbm.at[my_w], wrow, in_sem.at[0]),
        pltpu.make_async_copy(k_hbm, kv.at[0, pl.ds(4 * BLK, BLK)], in_sem.at[1]),
        pltpu.make_async_copy(v_hbm, kv.at[1, pl.ds(4 * BLK, BLK)], in_sem.at[2]),
        pltpu.make_async_copy(q_hbm, q, in_sem.at[3]),
    ]
    for copy in loads[:3]:
        copy.start()

    greet([sibling, partner, at_c(-2), at_c(-4)])
    greet([at_z(d, of_core) for d in (1, -1) for of_core in (0, 1)])

    @on_core(1)
    def _():
        greet([at_c(4)])
        greet([at_z(d, of_core) for d in range(2, NZ - 1) for of_core in (0, 1)])

    loads[3].start()

    def past_copies(j):
        rows = pl.ds(pl.multiple_of(jnp.minimum(c + j, 3) * BLK, BLK), BLK)
        return (
            pltpu.make_async_copy(pk_hbm.at[rows], kv.at[0, pl.ds(j * BLK, BLK)], past_sem.at[2 * j]),
            pltpu.make_async_copy(pv_hbm.at[rows], kv.at[1, pl.ds(j * BLK, BLK)], past_sem.at[2 * j + 1]),
        )

    def each_past(act):
        @pl.when(c < 4)
        def _():
            for j in range(4):
                @pl.when(c + j < 4)
                def _(j=j):
                    for copy in past_copies(j):
                        act(copy)

    each_past(lambda copy: copy.start())

    with jax.named_scope("weight_rows"):
        loads[0].wait()
    group = lax.broadcasted_iota(jnp.int32, (ROWS, 128), 1) // TAIL
    for t in range(NZ):
        d = lax.rem(z - t + NZ, NZ)
        s = jnp.where(d > 4, 2 * (NZ - d), jnp.maximum(2 * d - 1, 0))
        at = t * 2 * COLS
        for i in range(5):
            wsrc[s, i] = wrow[:, at + i * 128 : at + (i + 1) * 128]
        tail = jnp.concatenate([wrow[:, at + MAIN : at + 2 * COLS]] * 4, axis=1)
        wsrc[s, 5] = jnp.where(group == lax.rem(s, 4), tail, jnp.zeros_like(tail))
    loads[1].wait()
    loads[2].wait()
    with jax.named_scope("entry"):
        @on_core(0)
        def _():
            pl.semaphore_wait(barrier, 13)

        @on_core(1)
        def _():
            pl.semaphore_wait(barrier, 14)

    def remote(src, dst, send, recv, device):
        return pltpu.make_async_remote_copy(
            src_ref=src, dst_ref=dst, send_sem=send, recv_sem=recv, device_id=device, device_id_type=MESH
        )

    def kv_slot(j):
        return kv.at[:, pl.ds(pl.multiple_of(j * BLK, BLK), BLK)]

    def kv_copy(j, device, send):
        return remote(kv_slot(4), kv_slot(j), send, kv_recv.at[j], device)

    def kv_start(j, device, send):
        for i in range(2):
            remote(kv_slot(4).at[i], kv_slot(j).at[i], send, kv_recv.at[j], device).start()

    to_far = kv_copy(0, at_c(4), kv_send.at[0])
    to_near = kv_copy(2, at_c(2), kv_send.at[1])
    to_next = kv_copy(3, sibling, kv_send.at[2])

    @pl.when(c + 2 < n_ctx)
    def _():
        kv_start(2, at_c(2), kv_send.at[1])

    @pl.when(c + 4 < n_ctx)
    def _():
        kv_start(0, at_c(4), kv_send.at[0])

    @on_core(0)
    def _():
        to_next.start()

    def w1_copy(s, of_core):
        return remote(wsrc.at[s], wstage.at[of_core, s], w1_send.at[s], w1_recv.at[of_core * 8 + s], at_z(-DIST[s], 1))

    @on_core(0)
    def _():
        w1_copy(0, 0).start()

    for s in range(1, NZ):
        w1_copy(s, core).start()

    near_slot = jnp.where(core == 0, 1, 3)
    fwd_near = remote(kv_slot(2), kv_slot(near_slot), fwd_send.at[0], kv_recv.at[near_slot], sibling)
    fwd_far = remote(kv_slot(0), kv_slot(1), fwd_send.at[1], kv_recv.at[1], sibling)

    def arrived(j):
        return remote(kv_slot(j), kv_slot(j), kv_send.at[0], kv_recv.at[j], sibling)

    def w_slab(n, dy):
        row = pl.multiple_of(lax.rem(y + dy + NY, NY) * 32, 32)
        tiles = pl.ds(10, 11) if n % 2 else pl.ds(0, 10)
        return wfull.at[n // 2, tiles, pl.ds(row, 32)]

    def wy_sem(n, way, step):
        return n * 8 + (way + 1) // 2 * 4 + step - 1

    def wy_copy(n, way, step):
        slab = w_slab(n, -way * (step - 1))
        i = wy_sem(n, way, step)
        return remote(slab, slab, wy_send.at[i], wy_recv.at[i], at_c(4 * way))

    def wy_arrived(n, way, step):
        slab = w_slab(n, -way * step)
        i = wy_sem(n, way, step)
        return remote(slab, slab, wy_send.at[i], wy_recv.at[i], at_c(4 * way))

    def ws_copy(n, dy):
        slab = w_slab(n, dy)
        i = n * 8 + dy + 3
        return remote(slab, slab, ws_send.at[i], ws_recv.at[i], sibling)

    def last_way(part):
        return 1 if part == 0 else -1

    def w_start(n):
        part = n // 2
        for of_core in range(2):
            rows = pl.ds(pl.multiple_of(y * 32 + of_core * ROWS, ROWS), ROWS)

            def piece(j, i):
                own = part * 4 + j == 0 and of_core == 1
                return wsrc[0, i] if own else wstage[of_core, part * 4 + j, i]

            for j in (n % 2 * 2, n % 2 * 2 + 1):
                if part * 4 + j or of_core == 0:
                    w1_copy(part * 4 + j, of_core).wait_recv()
                for i in range(5):
                    wfull[part, j * 5 + i, rows] = piece(j, i)
            if n % 2:
                wfull[part, TILES - 1, rows] = piece(0, 5) + piece(1, 5) + piece(2, 5) + piece(3, 5)
        for way in (1, -1):
            wy_copy(n, way, 1).start()
        ws_copy(n, 0).start()

    def w_step(n, step):
        for way in (1, -1):
            if step == 4 and way != last_way(n % 2):
                continue
            wy_arrived(n, way, step).wait_recv()
            if step < 3 or (step == 3 and way == last_way(n % 2)):
                wy_copy(n, way, step + 1).start()
            ws_copy(n, 4 if step == 4 else -way * step).start()

    def weights(*todo):
        @on_core(1)
        def _():
            for n, step in todo:
                with jax.named_scope("weight_%d_hop_%d" % (n, step)):
                    w_step(n, step) if step else w_start(n)

    weights((0, 0))
    with jax.named_scope("far_block"):
        @pl.when(c >= 4)
        def _():
            arrived(0).wait_recv()

    @pl.when((c >= 4) & (core == 1))
    def _():
        fwd_far.start()

    weights((1, 0), (2, 0))
    with jax.named_scope("near_block"):
        @pl.when(c >= 2)
        def _():
            arrived(2).wait_recv()
            fwd_near.start()

    weights((3, 0), (0, 1))
    each_past(lambda copy: copy.wait())
    loads[3].wait()

    with jax.named_scope("passed_blocks"):
        @pl.when((c >= 1) | (core == 1))
        def _():
            arrived(3).wait_recv()

        @pl.when(c >= 3)
        def _():
            arrived(1).wait_recv()

    factor = QUERY_SCALAR ** (-0.5) * LOG2E
    row = lax.broadcasted_iota(jnp.int32, (HALF, HALF), 0)
    col = lax.broadcasted_iota(jnp.int32, (HALF, HALF), 1)

    def attend(half):
        rows = pl.ds(half * HALF, HALF)
        keys = kv[0, half * HALF : half * HALF + SPAN]
        values = kv[1, half * HALF : half * HALF + SPAN]
        for g in range(2):
            head = pl.ds(g * HEAD_DIM, HEAD_DIM)
            s = lax.dot_general(
                q[rows, head], keys, (((1,), (1,)), ((), ())), preferred_element_type=jnp.float32
            )
            s = jnp.concatenate(
                [
                    jnp.where(col > row, s[:, :HALF], -jnp.inf),
                    s[:, HALF : SPAN - HALF],
                    jnp.where(col <= row, s[:, SPAN - HALF :], -jnp.inf),
                ],
                axis=1,
            )
            m = jnp.max(s, axis=1, keepdims=True)
            p = jnp.exp2((s - m) * factor)
            total = jnp.sum(p, axis=1, keepdims=True)
            mixed = jnp.dot(p.astype(jnp.bfloat16), values, preferred_element_type=jnp.float32)
            att[core, 0, rows, head] = (mixed / total).astype(jnp.bfloat16)

    def rows_of(half):
        return pl.ds(half * HALF, HALF)

    def chunk_of(n):
        return pl.ds(n * CHUNK, CHUNK)

    def z1_copy(n, way, of_core):
        rows = chunk_of(n)
        k = n * 2 + (way + 1) // 2
        return remote(
            att.at[of_core, 0, rows], att.at[of_core, SLOT[-way], rows],
            z1_send.at[k], z1_recv.at[k * 2 + of_core], at_z(way, 0),
        )

    def z_copy(n, way, step, of_core):
        rows = chunk_of(n)
        i = ((n * 2 + (way + 1) // 2) * 2 + step - 2) * 2 + of_core
        return remote(
            att.at[of_core, SLOT[-way * (step - 1)], rows], att.at[of_core, SLOT[-way * step], rows],
            z_send.at[i], z_recv.at[i], at_z(way, 0),
        )

    def z4_copy(n, of_core):
        way = last_way(n % 2)
        rows = chunk_of(n)
        return remote(
            att.at[of_core, SLOT[-way * 3], rows], att.at[of_core, SLOT[4], rows],
            z4_send.at[n * 2 + of_core], z4_recv.at[n], at_z(way, of_core),
        )

    def zs_copy(n, slot):
        rows = chunk_of(n)
        i = n * 8 + slot
        return remote(att.at[1, slot, rows], att.at[1, slot, rows], zs_send.at[i], zs_recv.at[i], sibling)

    def z_step(n, step):
        for way in (-1, 1):
            for of_core in range(2):
                if step == 1:
                    z1_copy(n, way, of_core).wait_recv()
                else:
                    z_copy(n, way, step, of_core).wait_recv()
                if step < 3:
                    z_copy(n, way, step + 1, of_core).start()
                elif way == last_way(n % 2):
                    z4_copy(n, of_core).start()
            zs_copy(n, SLOT[-way * step]).start()

    for half in range(2):
        with jax.named_scope("attend_%d" % half):
            attend(half)
        for n in range(half * CHUNKS // 2, (half + 1) * CHUNKS // 2):
            for way in (1, -1):
                z1_copy(n, way, core).start()

    @on_core(0)
    def _():
        for step in range(1, 4):
            for n in range(CHUNKS):
                with jax.named_scope("attended_%d_hop_%d" % (n, step)):
                    z_step(n, step)
        with jax.named_scope("weights_from_core_1"):
            for n in range(4):
                for dy in range(-3, 5):
                    ws_copy(n, dy).wait_recv()

    weights(*[(n, step) for step in range(1, 5) for n in range(4) if (n, step) != (0, 1)])

    tail_of = lax.broadcasted_iota(jnp.int32, (HALF, 128), 1) // TAIL

    def project(half, slots):
        rows = rows_of(half)
        for s in slots:
            at = s % 4 * 5
            weight = jnp.concatenate(
                [wfull[s // 4, at + i] for i in range(5)] + [wfull[s // 4, TILES - 1]], axis=1
            )
            term = jnp.dot(att[core, s, rows, :], weight, preferred_element_type=jnp.float32)
            tail = jnp.where(tail_of == s % 4, term[:, MAIN:], 0.0)
            if s == 0:
                acc[rows, :MAIN] = term[:, :MAIN]
                acc[rows, MAIN:] = tail
            else:
                acc[rows, :MAIN] += term[:, :MAIN]
                acc[rows, MAIN:] += tail

    def x_copy(half):
        return remote(
            xsend.at[half], other_hbm.at[:, pl.ds(half * HALF, HALF)], x_send.at[half], x_recv.at[half], partner
        )

    def own_copy(half):
        mine = pl.ds(pl.multiple_of(x_lo * COLS, 16), COLS)
        return pltpu.make_async_copy(acc_t.at[half, mine], own_hbm.at[:, pl.ds(half * HALF, HALF)], own_sem.at[half])

    for half in range(2):
        rows = rows_of(half)
        with jax.named_scope("attended_from_core_0"):
            @on_core(1)
            def _(half=half):
                for n in range(half * CHUNKS // 2, (half + 1) * CHUNKS // 2):
                    for slot in range(1, 7):
                        zs_copy(n, slot).wait_recv()
        with jax.named_scope("project_%d" % half):
            project(half, range(7))
        with jax.named_scope("attended_%d_hop_4" % half):
            for n in range(half * CHUNKS // 2, (half + 1) * CHUNKS // 2):
                z4_copy(n, core).wait_recv()
        project(half, range(7, 8))
        tail = acc[rows, MAIN:].T
        acc_t[half, :MAIN] = acc[rows, :MAIN].T
        acc_t[half, MAIN:] = tail[:32] + tail[32:64] + tail[64:96] + tail[96:]
        theirs = pl.ds(pl.multiple_of((1 - x_lo) * COLS, 16), COLS)
        xsend[half] = acc_t[half, theirs].astype(jnp.bfloat16)
        x_copy(half).start()
        own_copy(half).start()

    with jax.named_scope("sent"):
        @pl.when(c + 2 < n_ctx)
        def _():
            to_near.wait_send()

        @pl.when(c + 4 < n_ctx)
        def _():
            to_far.wait_send()

        @pl.when(c >= 2)
        def _():
            fwd_near.wait_send()

        @pl.when((c >= 4) & (core == 1))
        def _():
            fwd_far.wait_send()

        for s in range(1, NZ):
            w1_copy(s, core).wait_send()
        for n in range(CHUNKS):
            for way in (1, -1):
                z1_copy(n, way, core).wait_send()

        @on_core(0)
        def _():
            to_next.wait_send()
            w1_copy(0, 0).wait_send()
            for n in range(CHUNKS):
                for of_core in range(2):
                    for way in (1, -1):
                        for step in (2, 3):
                            z_copy(n, way, step, of_core).wait_send()
                    z4_copy(n, of_core).wait_send()
                for slot in range(1, 7):
                    zs_copy(n, slot).wait_send()

        @on_core(1)
        def _():
            for n in range(4):
                for way in (1, -1):
                    for step in range(1, 5):
                        if step < 4 or way == last_way(n % 2):
                            wy_copy(n, way, step).wait_send()
                for dy in range(-3, 5):
                    ws_copy(n, dy).wait_send()

    with jax.named_scope("partner_sums"):
        for half in range(2):
            own_copy(half).wait()
            x_copy(half).wait()


def body(queries, key_states, value_states, past_keys, past_values, out_weight):
    bf16 = jnp.bfloat16
    dma = pltpu.SemaphoreType.DMA
    own, other = pl.pallas_call(
        kernel,
        out_shape=(jax.ShapeDtypeStruct((COLS, BLK), jnp.float32), jax.ShapeDtypeStruct((COLS, BLK), bf16)),
        in_specs=[pl.BlockSpec(memory_space=pl.ANY)] * 6,
        out_specs=(pl.BlockSpec(memory_space=pl.ANY),) * 2,
        scratch_shapes=[
            pltpu.VMEM((BLK, 2 * HEAD_DIM), bf16),
            pltpu.VMEM((2, KEYS, HEAD_DIM), bf16),
            pltpu.VMEM((ROWS, out_weight.shape[1]), bf16),
            pltpu.VMEM((NZ, 6, ROWS, 128), bf16),
            pltpu.VMEM((2, NZ, 6, ROWS, 128), bf16),
            pltpu.VMEM((2, TILES, BLK, 128), bf16),
            pltpu.VMEM((2, NZ, BLK, 2 * HEAD_DIM), bf16),
            pltpu.VMEM((BLK, MAIN + 128), jnp.float32),
            pltpu.VMEM((2, 2 * COLS, HALF), jnp.float32),
            pltpu.VMEM((2, COLS, HALF), bf16),
            dma((4,)), dma((8,)), dma((2,)), dma((3,)), dma((4,)), dma((2,)),
            dma((8,)), dma((16,)), dma((32,)), dma((32,)), dma((32,)), dma((32,)),
            dma((2 * CHUNKS,)), dma((4 * CHUNKS,)), dma((8 * CHUNKS,)), dma((8 * CHUNKS,)),
            dma((2 * CHUNKS,)), dma((CHUNKS,)), dma((8 * CHUNKS,)), dma((8 * CHUNKS,)), dma((2,)), dma((2,)),
        ],
        compiler_params=pltpu.CompilerParams(
            collective_id=0, has_side_effects=True, vmem_limit_bytes=63 * 1024 * 1024
        ),
        cost_estimate=pl.CostEstimate(flops=10**9, bytes_accessed=4 * 10**6, transcendentals=700000),
    )(queries, key_states, value_states, past_keys, past_values, out_weight)
    return (own + other.astype(jnp.float32)).astype(bf16).T


def solution(mesh):
    placed = (
        P("ctx", "head"),
        P("ctx", "head"),
        P("ctx", "head"),
        P(None, "head"),
        P(None, "head"),
        P("head", None),
    )
    return jax.shard_map(
        body, mesh=mesh, in_specs=placed, out_specs=P("ctx", "head"), check_vma=False
    )
```

time: 153 us -> 46.2 us (0.30)
  the two profiles are of different devices: /device:TPU:8 before, /device:TPU:4 now
where the time goes in v2:
time: 46.2 us; the launch traced here: 46.1 us
  Pallas kernels  44.4 us (96%)
  other arithmetic  1.73 us (4%)
    pallas_call x1, Pallas kernels, body(): pl.pallas_call(kernel, out_shape=(jax.ShapeDtypeStruct((COLS, BLK), jnp.f...  44.4 us
    transpose x1, other arithmetic, body(): return (own + other.astype(jnp.float32)).astype(bf16).T  1.73 us

profile of v2, /device:TPU:4, one launch (start us, length us, event | category | flops | bytes accessed | tf_op | source)
XLA Modules:
  0.0 46.1 jit_solution(12774951799999955177)
XLA Ops:
  0.0 44.4 %shard_map.64 = (f32[336,256]{1,0:T(8,128)}, bf16[336,256]{1,0:T(8,128)(2,1)}) custom-call(bf16[256,256]{1,0:T(8,128)(2,1)} %q_hbm.1, bf16[256,128]{1,0:T(8,128)(2,1)} %k_hbm.1, bf16[256,128]{1,0:T(8,128)(2,1)} %v_hbm.1, bf16[1024,128]{1,0:T(8,128)(2,1)} %pk_hbm.1, bf16[1024,128]{1,0:T(8,128)(2,1)} %pv_hbm.1, bf16[256,5376]{1,0:T(8,128)(2,1)} %w_hbm.1), custom_call_target="tpu_custom_call" | custom-call | flops 1000000000 | bytes 4000000 | tf_op jit(solution)/shard_map/pallas_call | solution.py:461
  44.4 1.7 %fusion = bf16[256,336]{0,1:T(8,128)(2,1)} fusion(f32[336,256]{1,0:T(8,128)} %get-tuple-element.7, bf16[336,256]{1,0:T(8,128)(2,1)} %get-tuple-element.8), kind=kLoop, calls=%fused_computation.1 | loop fusion | flops 258048 | bytes 688128 | tf_op jit(solution)/shard_map/transpose | solution.py:487

commit v3 on v2

--- a/solution.py
+++ b/solution.py
@@ -31,7 +31,7 @@
     q, kv, wrow, wsrc, wstage, wfull, att, acc, acc_t, xsend,
     in_sem, past_sem, own_sem, kv_send, kv_recv, fwd_send,
     w1_send, w1_recv, wy_send, wy_recv, ws_send, ws_recv,
-    z1_send, z1_recv, z_send, z_recv, z4_send, z4_recv, zs_send, zs_recv, x_send, x_recv,
+    z1_send, z_send, z_recv, z4_recv, zs_send, zs_recv, x_send, x_recv,
 ):
     c = lax.axis_index("ctx")
     h = lax.axis_index("head")
@@ -79,21 +79,14 @@
 
     loads[3].start()
 
-    def past_copies(j):
-        rows = pl.ds(pl.multiple_of(jnp.minimum(c + j, 3) * BLK, BLK), BLK)
-        return (
-            pltpu.make_async_copy(pk_hbm.at[rows], kv.at[0, pl.ds(j * BLK, BLK)], past_sem.at[2 * j]),
-            pltpu.make_async_copy(pv_hbm.at[rows], kv.at[1, pl.ds(j * BLK, BLK)], past_sem.at[2 * j + 1]),
-        )
-
     def each_past(act):
-        @pl.when(c < 4)
-        def _():
-            for j in range(4):
-                @pl.when(c + j < 4)
-                def _(j=j):
-                    for copy in past_copies(j):
-                        act(copy)
+        for first in range(4):
+            @pl.when(c == first)
+            def _(first=first):
+                there = pl.ds(first * BLK, (4 - first) * BLK)
+                here = pl.ds(0, (4 - first) * BLK)
+                act(pltpu.make_async_copy(pk_hbm.at[there], kv.at[0, here], past_sem.at[0]))
+                act(pltpu.make_async_copy(pv_hbm.at[there], kv.at[1, here], past_sem.at[1]))
 
     each_past(lambda copy: copy.start())
 
@@ -124,6 +117,9 @@
             src_ref=src, dst_ref=dst, send_sem=send, recv_sem=recv, device_id=device, device_id_type=MESH
         )
 
+    def all_of(ref, sem):
+        return remote(ref, ref, sem, sem, sibling)
+
     def kv_slot(j):
         return kv.at[:, pl.ds(pl.multiple_of(j * BLK, BLK), BLK)]
 
@@ -151,7 +147,7 @@
         to_next.start()
 
     def w1_copy(s, of_core):
-        return remote(wsrc.at[s], wstage.at[of_core, s], w1_send.at[s], w1_recv.at[of_core * 8 + s], at_z(-DIST[s], 1))
+        return remote(wsrc.at[s], wstage.at[s, of_core], w1_send, w1_recv.at[s // 2], at_z(-DIST[s], 1))
 
     @on_core(0)
     def _():
@@ -173,38 +169,39 @@
         return wfull.at[n // 2, tiles, pl.ds(row, 32)]
 
     def wy_sem(n, way, step):
-        return n * 8 + (way + 1) // 2 * 4 + step - 1
+        return n * 7 + (step - 1) * 2 + (way + 1) // 2 if step < 4 else n * 7 + 6
 
     def wy_copy(n, way, step):
         slab = w_slab(n, -way * (step - 1))
         i = wy_sem(n, way, step)
-        return remote(slab, slab, wy_send.at[i], wy_recv.at[i], at_c(4 * way))
+        return remote(slab, slab, wy_send, wy_recv.at[i], at_c(4 * way))
 
     def wy_arrived(n, way, step):
         slab = w_slab(n, -way * step)
         i = wy_sem(n, way, step)
-        return remote(slab, slab, wy_send.at[i], wy_recv.at[i], at_c(4 * way))
+        return remote(slab, slab, wy_send, wy_recv.at[i], at_c(4 * way))
 
     def ws_copy(n, dy):
         slab = w_slab(n, dy)
-        i = n * 8 + dy + 3
-        return remote(slab, slab, ws_send.at[i], ws_recv.at[i], sibling)
+        return remote(slab, slab, ws_send, ws_recv, sibling)
 
     def last_way(part):
         return 1 if part == 0 else -1
 
     def w_start(n):
         part = n // 2
+        if n == 0:
+            all_of(wsrc.at[pl.ds(0, 3)], w1_recv.at[0]).wait_recv()
+        else:
+            all_of(wstage.at[pl.ds(n * 2, 2)], w1_recv.at[n]).wait_recv()
         for of_core in range(2):
             rows = pl.ds(pl.multiple_of(y * 32 + of_core * ROWS, ROWS), ROWS)
 
             def piece(j, i):
                 own = part * 4 + j == 0 and of_core == 1
-                return wsrc[0, i] if own else wstage[of_core, part * 4 + j, i]
+                return wsrc[0, i] if own else wstage[part * 4 + j, of_core, i]
 
             for j in (n % 2 * 2, n % 2 * 2 + 1):
-                if part * 4 + j or of_core == 0:
-                    w1_copy(part * 4 + j, of_core).wait_recv()
                 for i in range(5):
                     wfull[part, j * 5 + i, rows] = piece(j, i)
             if n % 2:
@@ -229,23 +226,30 @@
                 with jax.named_scope("weight_%d_hop_%d" % (n, step)):
                     w_step(n, step) if step else w_start(n)
 
+    def far_block():
+        with jax.named_scope("far_block"):
+            @pl.when(c >= 4)
+            def _():
+                arrived(0).wait_recv()
+
+        @pl.when((c >= 4) & (core == 1))
+        def _():
+            fwd_far.start()
+
+    def near_block():
+        with jax.named_scope("near_block"):
+            @pl.when(c >= 2)
+            def _():
+                arrived(2).wait_recv()
+                fwd_near.start()
+
+    near_first = (core == 0) | (lax.rem(c // 2, 2) == 1)
     weights((0, 0))
-    with jax.named_scope("far_block"):
-        @pl.when(c >= 4)
-        def _():
-            arrived(0).wait_recv()
-
-    @pl.when((c >= 4) & (core == 1))
-    def _():
-        fwd_far.start()
-
+    pl.when(near_first)(near_block)
+    pl.when(jnp.logical_not(near_first))(far_block)
     weights((1, 0), (2, 0))
-    with jax.named_scope("near_block"):
-        @pl.when(c >= 2)
-        def _():
-            arrived(2).wait_recv()
-            fwd_near.start()
-
+    pl.when(near_first)(far_block)
+    pl.when(jnp.logical_not(near_first))(near_block)
     weights((3, 0), (0, 1))
     each_past(lambda copy: copy.wait())
     loads[3].wait()
@@ -292,20 +296,21 @@
     def chunk_of(n):
         return pl.ds(n * CHUNK, CHUNK)
 
+    def z_sem(n, way, step):
+        return (n * 3 + step - 1) * 2 + (way + 1) // 2
+
     def z1_copy(n, way, of_core):
         rows = chunk_of(n)
-        k = n * 2 + (way + 1) // 2
         return remote(
             att.at[of_core, 0, rows], att.at[of_core, SLOT[-way], rows],
-            z1_send.at[k], z1_recv.at[k * 2 + of_core], at_z(way, 0),
+            z1_send, z_recv.at[z_sem(n, way, 1)], at_z(way, 0),
         )
 
-    def z_copy(n, way, step, of_core):
+    def z_copy(n, way, step):
         rows = chunk_of(n)
-        i = ((n * 2 + (way + 1) // 2) * 2 + step - 2) * 2 + of_core
         return remote(
-            att.at[of_core, SLOT[-way * (step - 1)], rows], att.at[of_core, SLOT[-way * step], rows],
-            z_send.at[i], z_recv.at[i], at_z(way, 0),
+            att.at[:, SLOT[-way * (step - 1)], rows], att.at[:, SLOT[-way * step], rows],
+            z_send, z_recv.at[z_sem(n, way, step)], at_z(way, 0),
         )
 
     def z4_copy(n, of_core):
@@ -313,24 +318,21 @@
         rows = chunk_of(n)
         return remote(
             att.at[of_core, SLOT[-way * 3], rows], att.at[of_core, SLOT[4], rows],
-            z4_send.at[n * 2 + of_core], z4_recv.at[n], at_z(way, of_core),
+            z_send, z4_recv.at[n], at_z(way, of_core),
         )
 
     def zs_copy(n, slot):
         rows = chunk_of(n)
-        i = n * 8 + slot
-        return remote(att.at[1, slot, rows], att.at[1, slot, rows], zs_send.at[i], zs_recv.at[i], sibling)
+        return remote(att.at[1, slot, rows], att.at[1, slot, rows], zs_send, zs_recv.at[n * 2 // CHUNKS], sibling)
 
     def z_step(n, step):
         for way in (-1, 1):
-            for of_core in range(2):
-                if step == 1:
-                    z1_copy(n, way, of_core).wait_recv()
-                else:
-                    z_copy(n, way, step, of_core).wait_recv()
-                if step < 3:
-                    z_copy(n, way, step + 1, of_core).start()
-                elif way == last_way(n % 2):
+            here = att.at[:, SLOT[-way * step], chunk_of(n)]
+            all_of(here, z_recv.at[z_sem(n, way, step)]).wait_recv()
+            if step < 3:
+                z_copy(n, way, step + 1).start()
+            elif way == last_way(n % 2):
+                for of_core in range(2):
                     z4_copy(n, of_core).start()
             zs_copy(n, SLOT[-way * step]).start()
 
@@ -348,9 +350,7 @@
                 with jax.named_scope("attended_%d_hop_%d" % (n, step)):
                     z_step(n, step)
         with jax.named_scope("weights_from_core_1"):
-            for n in range(4):
-                for dy in range(-3, 5):
-                    ws_copy(n, dy).wait_recv()
+            all_of(wfull, ws_recv).wait_recv()
 
     weights(*[(n, step) for step in range(1, 5) for n in range(4) if (n, step) != (0, 1)])
 
@@ -386,9 +386,7 @@
         with jax.named_scope("attended_from_core_0"):
             @on_core(1)
             def _(half=half):
-                for n in range(half * CHUNKS // 2, (half + 1) * CHUNKS // 2):
-                    for slot in range(1, 7):
-                        zs_copy(n, slot).wait_recv()
+                all_of(att.at[1, pl.ds(1, 6), rows_of(half)], zs_recv.at[half]).wait_recv()
         with jax.named_scope("project_%d" % half):
             project(half, range(7))
         with jax.named_scope("attended_%d_hop_4" % half):
@@ -420,34 +418,20 @@
         def _():
             fwd_far.wait_send()
 
-        for s in range(1, NZ):
-            w1_copy(s, core).wait_send()
-        for n in range(CHUNKS):
-            for way in (1, -1):
-                z1_copy(n, way, core).wait_send()
+        all_of(att.at[0, pl.ds(0, 2)], z1_send).wait_send()
 
         @on_core(0)
         def _():
             to_next.wait_send()
-            w1_copy(0, 0).wait_send()
-            for n in range(CHUNKS):
-                for of_core in range(2):
-                    for way in (1, -1):
-                        for step in (2, 3):
-                            z_copy(n, way, step, of_core).wait_send()
-                    z4_copy(n, of_core).wait_send()
-                for slot in range(1, 7):
-                    zs_copy(n, slot).wait_send()
+            all_of(wsrc, w1_send).wait_send()
+            all_of(att.at[:, pl.ds(0, 5)], z_send).wait_send()
+            all_of(att.at[1, pl.ds(0, 6)], zs_send).wait_send()
 
         @on_core(1)
         def _():
-            for n in range(4):
-                for way in (1, -1):
-                    for step in range(1, 5):
-                        if step < 4 or way == last_way(n % 2):
-                            wy_copy(n, way, step).wait_send()
-                for dy in range(-3, 5):
-                    ws_copy(n, dy).wait_send()
+            all_of(wsrc.at[pl.ds(0, 7)], w1_send).wait_send()
+            all_of(wfull.at[:, :, pl.ds(0, 7 * 32)], wy_send).wait_send()
+            all_of(wfull, ws_send).wait_send()
 
     with jax.named_scope("partner_sums"):
         for half in range(2):
@@ -468,16 +452,15 @@
             pltpu.VMEM((2, KEYS, HEAD_DIM), bf16),
             pltpu.VMEM((ROWS, out_weight.shape[1]), bf16),
             pltpu.VMEM((NZ, 6, ROWS, 128), bf16),
-            pltpu.VMEM((2, NZ, 6, ROWS, 128), bf16),
+            pltpu.VMEM((NZ, 2, 6, ROWS, 128), bf16),
             pltpu.VMEM((2, TILES, BLK, 128), bf16),
             pltpu.VMEM((2, NZ, BLK, 2 * HEAD_DIM), bf16),
             pltpu.VMEM((BLK, MAIN + 128), jnp.float32),
             pltpu.VMEM((2, 2 * COLS, HALF), jnp.float32),
             pltpu.VMEM((2, COLS, HALF), bf16),
-            dma((4,)), dma((8,)), dma((2,)), dma((3,)), dma((4,)), dma((2,)),
-            dma((8,)), dma((16,)), dma((32,)), dma((32,)), dma((32,)), dma((32,)),
-            dma((2 * CHUNKS,)), dma((4 * CHUNKS,)), dma((8 * CHUNKS,)), dma((8 * CHUNKS,)),
-            dma((2 * CHUNKS,)), dma((CHUNKS,)), dma((8 * CHUNKS,)), dma((8 * CHUNKS,)), dma((2,)), dma((2,)),
+            dma((4,)), dma((2,)), dma((2,)), dma((3,)), dma((4,)), dma((2,)),
+            dma(()), dma((4,)), dma(()), dma((28,)), dma(()), dma(()),
+            dma(()), dma(()), dma((6 * CHUNKS,)), dma((CHUNKS,)), dma(()), dma((2,)), dma((2,)), dma((2,)),
         ],
         compiler_params=pltpu.CompilerParams(
             collective_id=0, has_side_effects=True, vmem_limit_bytes=63 * 1024 * 1024

time: 46.2 us -> 43.3 us (0.937)
  the two profiles are of different devices: /device:TPU:4 before, /device:TPU:24 now
where the time goes in v3:
time: 43.3 us; the launch traced here: 43.1 us
  Pallas kernels  41.4 us (96%)
  other arithmetic  1.73 us (4%)
    pallas_call x1, Pallas kernels, body(): pl.pallas_call(kernel, out_shape=(jax.ShapeDtypeStruct((COLS, BLK), jnp.f...  41.4 us
    transpose x1, other arithmetic, body(): return (own + other.astype(jnp.float32)).astype(bf16).T  1.73 us

profile of v3, /device:TPU:24, one launch (start us, length us, event | category | flops | bytes accessed | tf_op | source)
XLA Modules:
  0.0 43.1 jit_solution(815419601107724763)
XLA Ops:
  0.0 41.4 %shard_map.64 = (f32[336,256]{1,0:T(8,128)}, bf16[336,256]{1,0:T(8,128)(2,1)}) custom-call(bf16[256,256]{1,0:T(8,128)(2,1)} %q_hbm.1, bf16[256,128]{1,0:T(8,128)(2,1)} %k_hbm.1, bf16[256,128]{1,0:T(8,128)(2,1)} %v_hbm.1, bf16[1024,128]{1,0:T(8,128)(2,1)} %pk_hbm.1, bf16[1024,128]{1,0:T(8,128)(2,1)} %pv_hbm.1, bf16[256,5376]{1,0:T(8,128)(2,1)} %w_hbm.1), custom_call_target="tpu_custom_call" | custom-call | flops 1000000000 | bytes 4000000 | tf_op jit(solution)/shard_map/pallas_call | solution.py:445
  41.4 1.7 %fusion = bf16[256,336]{0,1:T(8,128)(2,1)} fusion(f32[336,256]{1,0:T(8,128)} %get-tuple-element.7, bf16[336,256]{1,0:T(8,128)(2,1)} %get-tuple-element.8), kind=kLoop, calls=%fused_computation.1 | loop fusion | flops 258048 | bytes 688128 | tf_op jit(solution)/shard_map/transpose | solution.py:470

commit v4 on v3

--- a/solution.py
+++ b/solution.py
@@ -66,9 +66,6 @@
         pltpu.make_async_copy(v_hbm, kv.at[1, pl.ds(4 * BLK, BLK)], in_sem.at[2]),
         pltpu.make_async_copy(q_hbm, q, in_sem.at[3]),
     ]
-    for copy in loads[:3]:
-        copy.start()
-
     greet([sibling, partner, at_c(-2), at_c(-4)])
     greet([at_z(d, of_core) for d in (1, -1) for of_core in (0, 1)])
 
@@ -77,7 +74,8 @@
         greet([at_c(4)])
         greet([at_z(d, of_core) for d in range(2, NZ - 1) for of_core in (0, 1)])
 
-    loads[3].start()
+    for copy in loads:
+        copy.start()
 
     def each_past(act):
         for first in range(4):
@@ -264,31 +262,30 @@
             arrived(1).wait_recv()
 
     factor = QUERY_SCALAR ** (-0.5) * LOG2E
-    row = lax.broadcasted_iota(jnp.int32, (HALF, HALF), 0)
-    col = lax.broadcasted_iota(jnp.int32, (HALF, HALF), 1)
+    row = lax.rem(lax.broadcasted_iota(jnp.int32, (2 * HALF, HALF), 0), HALF)
+    col = lax.broadcasted_iota(jnp.int32, (2 * HALF, HALF), 1)
 
     def attend(half):
         rows = pl.ds(half * HALF, HALF)
         keys = kv[0, half * HALF : half * HALF + SPAN]
         values = kv[1, half * HALF : half * HALF + SPAN]
-        for g in range(2):
-            head = pl.ds(g * HEAD_DIM, HEAD_DIM)
-            s = lax.dot_general(
-                q[rows, head], keys, (((1,), (1,)), ((), ())), preferred_element_type=jnp.float32
-            )
-            s = jnp.concatenate(
-                [
-                    jnp.where(col > row, s[:, :HALF], -jnp.inf),
-                    s[:, HALF : SPAN - HALF],
-                    jnp.where(col <= row, s[:, SPAN - HALF :], -jnp.inf),
-                ],
-                axis=1,
-            )
-            m = jnp.max(s, axis=1, keepdims=True)
-            p = jnp.exp2((s - m) * factor)
-            total = jnp.sum(p, axis=1, keepdims=True)
-            mixed = jnp.dot(p.astype(jnp.bfloat16), values, preferred_element_type=jnp.float32)
-            att[core, 0, rows, head] = (mixed / total).astype(jnp.bfloat16)
+        both = jnp.concatenate([q[rows, :HEAD_DIM], q[rows, HEAD_DIM:]], axis=0)
+        s = lax.dot_general(both, keys, (((1,), (1,)), ((), ())), preferred_element_type=jnp.float32)
+        s = jnp.concatenate(
+            [
+                jnp.where(col > row, s[:, :HALF], -jnp.inf),
+                s[:, HALF : SPAN - HALF],
+                jnp.where(col <= row, s[:, SPAN - HALF :], -jnp.inf),
+            ],
+            axis=1,
+        )
+        m = jnp.max(s, axis=1, keepdims=True)
+        p = jnp.exp2((s - m) * factor)
+        total = jnp.sum(p, axis=1, keepdims=True)
+        mixed = jnp.dot(p.astype(jnp.bfloat16), values, preferred_element_type=jnp.float32)
+        mixed = (mixed * (1.0 / total)).astype(jnp.bfloat16)
+        att[core, 0, rows, :HEAD_DIM] = mixed[:HALF]
+        att[core, 0, rows, HEAD_DIM:] = mixed[HALF:]
 
     def rows_of(half):
         return pl.ds(half * HALF, HALF)

time: 43.3 us -> 43.2 us (level)
  the two profiles are of different devices: /device:TPU:24 before, /device:TPU:16 now
where the time goes in v4:
time: 43.2 us; the launch traced here: 43 us
  Pallas kernels  41.3 us (96%)
  other arithmetic  1.73 us (4%)
    pallas_call x1, Pallas kernels, body(): pl.pallas_call(kernel, out_shape=(jax.ShapeDtypeStruct((COLS, BLK), jnp.f...  41.3 us
    transpose x1, other arithmetic, body(): return (own + other.astype(jnp.float32)).astype(bf16).T  1.73 us

profile of v4, /device:TPU:16, one launch (start us, length us, event | category | flops | bytes accessed | tf_op | source)
XLA Modules:
  0.0 43.0 jit_solution(16556702071968655975)
XLA Ops:
  0.0 41.3 %shard_map.64 = (f32[336,256]{1,0:T(8,128)}, bf16[336,256]{1,0:T(8,128)(2,1)}) custom-call(bf16[256,256]{1,0:T(8,128)(2,1)} %q_hbm.1, bf16[256,128]{1,0:T(8,128)(2,1)} %k_hbm.1, bf16[256,128]{1,0:T(8,128)(2,1)} %v_hbm.1, bf16[1024,128]{1,0:T(8,128)(2,1)} %pk_hbm.1, bf16[1024,128]{1,0:T(8,128)(2,1)} %pv_hbm.1, bf16[256,5376]{1,0:T(8,128)(2,1)} %w_hbm.1), custom_call_target="tpu_custom_call" | custom-call | flops 1000000000 | bytes 4000000 | tf_op jit(solution)/shard_map/pallas_call | solution.py:442
  41.3 1.7 %fusion = bf16[256,336]{0,1:T(8,128)(2,1)} fusion(f32[336,256]{1,0:T(8,128)} %get-tuple-element.7, bf16[336,256]{1,0:T(8,128)(2,1)} %get-tuple-element.8), kind=kLoop, calls=%fused_computation.1 | loop fusion | flops 258048 | bytes 688128 | tf_op jit(solution)/shard_map/transpose | solution.py:467

commit v5 on v4

--- a/solution.py
+++ b/solution.py
@@ -29,7 +29,7 @@
 def kernel(
     q_hbm, k_hbm, v_hbm, pk_hbm, pv_hbm, w_hbm, own_hbm, other_hbm,
     q, kv, wrow, wsrc, wstage, wfull, att, acc, acc_t, xsend,
-    in_sem, past_sem, own_sem, kv_send, kv_recv, fwd_send,
+    z_ready, next_ready, in_sem, past_sem, own_sem, kv_send, kv_recv, fwd_send,
     w1_send, w1_recv, wy_send, wy_recv, ws_send, ws_recv,
     z1_send, z_send, z_recv, z4_recv, zs_send, zs_recv, x_send, x_recv,
 ):
@@ -67,12 +67,32 @@
         pltpu.make_async_copy(q_hbm, q, in_sem.at[3]),
     ]
     greet([sibling, partner, at_c(-2), at_c(-4)])
-    greet([at_z(d, of_core) for d in (1, -1) for of_core in (0, 1)])
+
+    def cores_at(t):
+        return [(c0 + of_core, t * 2 + x_lo) for of_core in range(2)]
+
+    @on_core(0)
+    def _():
+        @pl.when(z < NZ - 1)
+        def _():
+            greet(cores_at(z + 1)[:1])
+
+        @pl.when(z == 0)
+        def _():
+            greet(cores_at(NZ - 1)[:1])
+
+        for t in range(1, NZ):
+            @pl.when(z < t)
+            def _(t=t):
+                greet(cores_at(t)[1:])
 
     @on_core(1)
     def _():
         greet([at_c(4)])
-        greet([at_z(d, of_core) for d in range(2, NZ - 1) for of_core in (0, 1)])
+        for t in range(1, NZ):
+            @pl.when(z < t)
+            def _(t=t):
+                greet(cores_at(t))
 
     for copy in loads:
         copy.start()
@@ -102,13 +122,29 @@
     loads[1].wait()
     loads[2].wait()
     with jax.named_scope("entry"):
-        @on_core(0)
-        def _():
-            pl.semaphore_wait(barrier, 13)
-
-        @on_core(1)
-        def _():
-            pl.semaphore_wait(barrier, 14)
+        neighbours = jnp.where(z >= 1, 1, 0) + jnp.where(z == NZ - 1, 1, 0)
+        pl.semaphore_wait(barrier, jnp.where(core == 0, 4 + z + neighbours, 5 + 2 * z))
+
+    def ready(sem, devices):
+        for device in devices:
+            pl.semaphore_signal(sem, inc=1, device_id=device, device_id_type=MESH)
+
+    @on_core(0)
+    def _():
+        @pl.when(z >= 1)
+        def _():
+            ready(next_ready.at[0], cores_at(z - 1))
+
+        @pl.when(z == NZ - 1)
+        def _():
+            ready(next_ready.at[1], cores_at(0))
+
+    @on_core(1)
+    def _():
+        for t in range(NZ - 1):
+            @pl.when(t < z)
+            def _(t=t):
+                ready(z_ready.at[z], cores_at(t))
 
     def remote(src, dst, send, recv, device):
         return pltpu.make_async_remote_copy(
@@ -151,8 +187,23 @@
     def _():
         w1_copy(0, 0).start()
 
-    for s in range(1, NZ):
-        w1_copy(s, core).start()
+    def rounded_up(s):
+        return DIST[s] if DIST[s] > 0 else NZ + DIST[s]
+
+    def w1_below():
+        for s in range(1, NZ):
+            @pl.when(z >= rounded_up(s))
+            def _(s=s):
+                w1_copy(s, core).start()
+
+    def w1_above(slots):
+        for s in slots:
+            @pl.when(z < rounded_up(s))
+            def _(s=s):
+                pl.semaphore_wait(z_ready.at[z + NZ - rounded_up(s)], 1)
+                w1_copy(s, core).start()
+
+    w1_below()
 
     near_slot = jnp.where(core == 0, 1, 3)
     fwd_near = remote(kv_slot(2), kv_slot(near_slot), fwd_send.at[0], kv_recv.at[near_slot], sibling)
@@ -242,13 +293,13 @@
                 fwd_near.start()
 
     near_first = (core == 0) | (lax.rem(c // 2, 2) == 1)
-    weights((0, 0))
+    pl.when(z < NZ - 1)(lambda: weights((0, 0)))
     pl.when(near_first)(near_block)
     pl.when(jnp.logical_not(near_first))(far_block)
-    weights((1, 0), (2, 0))
+    w1_above((2, 4, 6))
     pl.when(near_first)(far_block)
     pl.when(jnp.logical_not(near_first))(near_block)
-    weights((3, 0), (0, 1))
+    pl.when(z >= 2)(lambda: w1_above((7, 5)))
     each_past(lambda copy: copy.wait())
     loads[3].wait()
 
@@ -336,9 +387,20 @@
     for half in range(2):
         with jax.named_scope("attend_%d" % half):
             attend(half)
+        if half == 0:
+            with jax.named_scope("next_ready"):
+                @pl.when(z < NZ - 1)
+                def _():
+                    pl.semaphore_wait(next_ready.at[0], 1)
+
+                @pl.when(z == 0)
+                def _():
+                    pl.semaphore_wait(next_ready.at[1], 1)
         for n in range(half * CHUNKS // 2, (half + 1) * CHUNKS // 2):
             for way in (1, -1):
                 z1_copy(n, way, core).start()
+    with jax.named_scope("weight_rows_up"):
+        pl.when(z < 2)(lambda: w1_above((7, 5, 3, 1)))
 
     @on_core(0)
     def _():
@@ -349,7 +411,13 @@
         with jax.named_scope("weights_from_core_1"):
             all_of(wfull, ws_recv).wait_recv()
 
-    weights(*[(n, step) for step in range(1, 5) for n in range(4) if (n, step) != (0, 1)])
+    pl.when(z == 0)(lambda: weights((2, 0), (3, 0), (1, 0), *[(n, step) for step in range(1, 5) for n in (0, 2, 3, 1)]))
+
+    @pl.when(z > 0)
+    def _():
+        pl.when(z == NZ - 1)(lambda: weights((0, 0)))
+        weights((1, 0), (2, 0), (3, 0), *[(n, step) for step in range(1, 5) for n in range(4)])
+
 
     tail_of = lax.broadcasted_iota(jnp.int32, (HALF, 128), 1) // TAIL
 
@@ -455,6 +523,7 @@
             pltpu.VMEM((BLK, MAIN + 128), jnp.float32),
             pltpu.VMEM((2, 2 * COLS, HALF), jnp.float32),
             pltpu.VMEM((2, COLS, HALF), bf16),
+            pltpu.SemaphoreType.REGULAR((8,)), pltpu.SemaphoreType.REGULAR((2,)),
             dma((4,)), dma((2,)), dma((2,)), dma((3,)), dma((4,)), dma((2,)),
             dma(()), dma((4,)), dma(()), dma((28,)), dma(()), dma(()),
             dma(()), dma(()), dma((6 * CHUNKS,)), dma((CHUNKS,)), dma(()), dma((2,)), dma((2,)), dma((2,)),

time: 43.2 us -> 42.7 us (0.988)
  the two profiles are of different devices: /device:TPU:16 before, /device:TPU:32 now
where the time goes in v5:
time: 42.7 us; the launch traced here: 42.2 us
  Pallas kernels  40.5 us (95%)
  other arithmetic  1.73 us (4%)
    pallas_call x1, Pallas kernels, body(): pl.pallas_call(kernel, out_shape=(jax.ShapeDtypeStruct((COLS, BLK), jnp.f...  40.5 us
    transpose x1, other arithmetic, body(): return (own + other.astype(jnp.float32)).astype(bf16).T  1.73 us

profile of v5, /device:TPU:32, one launch (start us, length us, event | category | flops | bytes accessed | tf_op | source)
XLA Modules:
  0.0 42.2 jit_solution(15901485319284334080)
XLA Ops:
  0.0 40.5 %shard_map.64 = (f32[336,256]{1,0:T(8,128)}, bf16[336,256]{1,0:T(8,128)(2,1)}) custom-call(bf16[256,256]{1,0:T(8,128)(2,1)} %q_hbm.1, bf16[256,128]{1,0:T(8,128)(2,1)} %k_hbm.1, bf16[256,128]{1,0:T(8,128)(2,1)} %v_hbm.1, bf16[1024,128]{1,0:T(8,128)(2,1)} %pk_hbm.1, bf16[1024,128]{1,0:T(8,128)(2,1)} %pv_hbm.1, bf16[256,5376]{1,0:T(8,128)(2,1)} %w_hbm.1), custom_call_target="tpu_custom_call" | custom-call | flops 1000000000 | bytes 4000000 | tf_op jit(solution)/shard_map/pallas_call | solution.py:510
  40.5 1.7 %fusion = bf16[256,336]{0,1:T(8,128)(2,1)} fusion(f32[336,256]{1,0:T(8,128)} %get-tuple-element.7, bf16[336,256]{1,0:T(8,128)(2,1)} %get-tuple-element.8), kind=kLoop, calls=%fused_computation.1 | loop fusion | flops 258048 | bytes 688128 | tf_op jit(solution)/shard_map/transpose | solution.py:536

commit v6 on v5

--- a/solution.py
+++ b/solution.py
@@ -388,6 +388,7 @@
         with jax.named_scope("attend_%d" % half):
             attend(half)
         if half == 0:
+            pl.when(z < 2)(lambda: w1_above((1, 3, 5, 7)))
             with jax.named_scope("next_ready"):
                 @pl.when(z < NZ - 1)
                 def _():
@@ -399,8 +400,6 @@
         for n in range(half * CHUNKS // 2, (half + 1) * CHUNKS // 2):
             for way in (1, -1):
                 z1_copy(n, way, core).start()
-    with jax.named_scope("weight_rows_up"):
-        pl.when(z < 2)(lambda: w1_above((7, 5, 3, 1)))
 
     @on_core(0)
     def _():

time: 42.7 us -> 42.3 us (level)
  no operation moved by 1% of the time
where the time goes in v6:
time: 42.3 us; the launch traced here: 42.2 us
  Pallas kernels  40.5 us (96%)
  other arithmetic  1.73 us (4%)
    pallas_call x1, Pallas kernels, body(): pl.pallas_call(kernel, out_shape=(jax.ShapeDtypeStruct((COLS, BLK), jnp.f...  40.5 us
    transpose x1, other arithmetic, body(): return (own + other.astype(jnp.float32)).astype(bf16).T  1.73 us

profile of v6, /device:TPU:32, one launch (start us, length us, event | category | flops | bytes accessed | tf_op | source)
XLA Modules:
  0.0 42.2 jit_solution(14304528738386686352)
XLA Ops:
  0.0 40.5 %shard_map.64 = (f32[336,256]{1,0:T(8,128)}, bf16[336,256]{1,0:T(8,128)(2,1)}) custom-call(bf16[256,256]{1,0:T(8,128)(2,1)} %q_hbm.1, bf16[256,128]{1,0:T(8,128)(2,1)} %k_hbm.1, bf16[256,128]{1,0:T(8,128)(2,1)} %v_hbm.1, bf16[1024,128]{1,0:T(8,128)(2,1)} %pk_hbm.1, bf16[1024,128]{1,0:T(8,128)(2,1)} %pv_hbm.1, bf16[256,5376]{1,0:T(8,128)(2,1)} %w_hbm.1), custom_call_target="tpu_custom_call" | custom-call | flops 1000000000 | bytes 4000000 | tf_op jit(solution)/shard_map/pallas_call | solution.py:509
  40.5 1.7 %fusion = bf16[256,336]{0,1:T(8,128)(2,1)} fusion(f32[336,256]{1,0:T(8,128)} %get-tuple-element.7, bf16[336,256]{1,0:T(8,128)(2,1)} %get-tuple-element.8), kind=kLoop, calls=%fused_computation.1 | loop fusion | flops 258048 | bytes 688128 | tf_op jit(solution)/shard_map/transpose | solution.py:535

commit v7 on v6

--- a/solution.py
+++ b/solution.py
@@ -373,8 +373,8 @@
         rows = chunk_of(n)
         return remote(att.at[1, slot, rows], att.at[1, slot, rows], zs_send, zs_recv.at[n * 2 // CHUNKS], sibling)
 
-    def z_step(n, step):
-        for way in (-1, 1):
+    def z_step(n, step, ways):
+        for way in ways:
             here = att.at[:, SLOT[-way * step], chunk_of(n)]
             all_of(here, z_recv.at[z_sem(n, way, step)]).wait_recv()
             if step < 3:
@@ -401,12 +401,16 @@
             for way in (1, -1):
                 z1_copy(n, way, core).start()
 
-    @on_core(0)
-    def _():
+    def z_steps(ways):
         for step in range(1, 4):
             for n in range(CHUNKS):
                 with jax.named_scope("attended_%d_hop_%d" % (n, step)):
-                    z_step(n, step)
+                    z_step(n, step, ways)
+
+    @on_core(0)
+    def _():
+        pl.when(z == 0)(lambda: z_steps((-1, 1)))
+        pl.when(z > 0)(lambda: z_steps((1, -1)))
         with jax.named_scope("weights_from_core_1"):
             all_of(wfull, ws_recv).wait_recv()
 

time: 42.3 us -> 42.9 us (1.014)
    pallas_call x1, Pallas kernels: 40.5 us -> 40.9 us  [body(): pl.pallas_call(kernel, out_shape=(jax.ShapeDtypeStruct((COLS, BLK), jnp.f...]
where the time goes in v7:
time: 42.9 us; the launch traced here: 42.7 us
  Pallas kernels  40.9 us (95%)
  other arithmetic  1.73 us (4%)
    pallas_call x1, Pallas kernels, body(): pl.pallas_call(kernel, out_shape=(jax.ShapeDtypeStruct((COLS, BLK), jnp.f...  40.9 us
    transpose x1, other arithmetic, body(): return (own + other.astype(jnp.float32)).astype(bf16).T  1.73 us

profile of v7, /device:TPU:32, one launch (start us, length us, event | category | flops | bytes accessed | tf_op | source)
XLA Modules:
  0.0 42.7 jit_solution(15107986650664603657)
XLA Ops:
  0.0 40.9 %shard_map.64 = (f32[336,256]{1,0:T(8,128)}, bf16[336,256]{1,0:T(8,128)(2,1)}) custom-call(bf16[256,256]{1,0:T(8,128)(2,1)} %q_hbm.1, bf16[256,128]{1,0:T(8,128)(2,1)} %k_hbm.1, bf16[256,128]{1,0:T(8,128)(2,1)} %v_hbm.1, bf16[1024,128]{1,0:T(8,128)(2,1)} %pk_hbm.1, bf16[1024,128]{1,0:T(8,128)(2,1)} %pv_hbm.1, bf16[256,5376]{1,0:T(8,128)(2,1)} %w_hbm.1), custom_call_target="tpu_custom_call" | custom-call | flops 1000000000 | bytes 4000000 | tf_op jit(solution)/shard_map/pallas_call | solution.py:513
  41.0 1.7 %fusion = bf16[256,336]{0,1:T(8,128)(2,1)} fusion(f32[336,256]{1,0:T(8,128)} %get-tuple-element.7, bf16[336,256]{1,0:T(8,128)(2,1)} %get-tuple-element.8), kind=kLoop, calls=%fused_computation.1 | loop fusion | flops 258048 | bytes 688128 | tf_op jit(solution)/shard_map/transpose | solution.py:539
